TPU v7x, 32 devices: a whole 2x2x4 slice. The times are simulated.
32 devices in a mesh: slab: 8 (over z, y), disk: 4 (over x, core).
Axes of the slice: x: 2, y: 2, z: 4, core: 2. Of those that a mesh axis runs over, the one named last changes fastest.
Arguments:
- thermal_anomaly: float32 [2, 8, 1024], P(None, 'slab', 'disk'), may hold values from 0.5 to 1.5
- humidity_amount: float32 [2, 8, 1024], P(None, 'slab', 'disk'), may hold values from 0.2 to 2
- slab_condensate_amount: float32 [2, 8, 1024], P(None, 'slab', 'disk'), may hold values from 0.1 to 2
- overcast_indicator: int32 [2, 1024], P(None, 'disk'), may hold values 0 or 1
- molecular_opacity: float32 [112, 8], replicated, may hold values from 0.003 to 0.1
- condensate_opacity: float32 [112], replicated, may hold values from 0.01 to 0.1
- planck_quadrature_factor: float32 [112], replicated, may hold values from 0.5 to 2
- scene_contributing_profiles: int32 [4, 16384], P(None, ('slab', 'disk')), may hold values from 0 to 1023, as said below
- scene_interpolation_factors: float32 [4, 16384], P(None, ('slab', 'disk')), may hold values from 0.1 to 1
Outputs:
- pixel_radiance: float32 [2, 16, 16384], P(None, None, ('slab', 'disk'))
Inputs may be any that keep to these rules, and one draw needn't show every extreme that they name: `scene_contributing_profiles`: every source column c of pixel p lies in the pixel's latitude strip: (c % 256) // 32 == p // 2048.
All inputs are finite; a program needn't handle non-finite values. No bound on the sum of `overcast_indicator` on one device may be relied on, other than what follows from the above.
Results may differ from a plain program's by a relative error of at most 0.0017.
Values may be sent and summed in bfloat16 or wider, within the bound.
A program may use at most 64 MiB of HBM per device.

v0:
```python
import jax
import jax.numpy as jnp
from jax import lax
from jax.sharding import PartitionSpec as P

BANDS = 16
GPB = 7


def band_block(
    temp_four, vapour_cols, cloud_cols, gas_band, cloud_band, planck_band, upper_level_mask
):
    optical_depth = (
        gas_band[:, :, None] * vapour_cols[None] + cloud_band[:, None, None] * cloud_cols[None]
    )
    optical_depth_above = jnp.einsum(
        "vh,qha->qva", upper_level_mask, optical_depth, precision=lax.Precision.HIGHEST
    )
    planck = planck_band[:, None, None] * temp_four[None]
    visible = jnp.exp(-optical_depth_above)
    emitted = jnp.sum(planck * visible * (1.0 - jnp.exp(-optical_depth)), axis=1)
    ground = planck[:, -1] * visible[:, -1] * jnp.exp(-optical_depth[:, -1])
    return jnp.sum(emitted + ground, axis=0) / gas_band.shape[0]


def local(
    thermal_anomaly,
    humidity_amount,
    slab_condensate_amount,
    overcast_indicator,
    molecular_opacity,
    condensate_opacity,
    planck_quadrature_factor,
    scene_contributing_profiles,
    scene_interpolation_factors,
):
    level_count = molecular_opacity.shape[1]
    level_index = jnp.arange(level_count)
    upper_level_mask = (level_index[None, :] < level_index[:, None]).astype(jnp.float32)
    gas_bands = molecular_opacity.reshape(BANDS, GPB, level_count)
    cloud_bands = condensate_opacity.reshape(BANDS, GPB)
    planck_bands = planck_quadrature_factor.reshape(BANDS, GPB)
    overcast_fraction_intensity = (
        slab_condensate_amount * overcast_indicator.astype(jnp.float32)[:, None, :]
    )

    def radiate(pieces):
        temp_four = pieces[0] ** 4

        def one_band(coeffs):
            return band_block(
                temp_four, pieces[1], pieces[2], coeffs[0], coeffs[1], coeffs[2], upper_level_mask
            )

        return lax.map(one_band, (gas_bands, cloud_bands, planck_bands)).astype(jnp.bfloat16)

    fields = (
        lax.all_to_all(thermal_anomaly, "slab", split_axis=2, concat_axis=1, tiled=True),
        lax.all_to_all(humidity_amount, "slab", split_axis=2, concat_axis=1, tiled=True),
        lax.all_to_all(
            overcast_fraction_intensity, "slab", split_axis=2, concat_axis=1, tiled=True
        ),
    )
    spectral_interval_intensity = lax.map(radiate, fields)
    block_cols = spectral_interval_intensity.shape[2]
    sector_cols = block_cols * lax.axis_size("slab")
    strip_rad = lax.all_gather(spectral_interval_intensity, "disk", axis=2, tiled=True)
    strip_index = (
        scene_contributing_profiles // sector_cols * block_cols
        + scene_contributing_profiles % block_cols
    )
    picked = strip_rad[:, :, strip_index].astype(jnp.float32)
    pixels = jnp.sum(picked * scene_interpolation_factors[None, None], axis=2)
    return pixels


def solution(mesh):
    in_specs = (
        P(None, "slab", "disk"),
        P(None, "slab", "disk"),
        P(None, "slab", "disk"),
        P(None, "disk"),
        P(),
        P(),
        P(),
        P(None, ("slab", "disk")),
        P(None, ("slab", "disk")),
    )
    out_specs = P(None, None, ("slab", "disk"))
    return jax.shard_map(local, mesh=mesh, in_specs=in_specs, out_specs=out_specs, check_vma=False)
```

profile of v0, /device:TPU:0, one launch (start us, length us, event | category | flops | bytes accessed | tf_op | source)
XLA Modules:
  0.0 70.0 jit_solution(9951289085315843617)
XLA Ops:
  0.0 0.0 copy-start.2
  0.0 1.5 %copy.39 = f32[2,1,256]{0,1,2:T(1,128)} copy(f32[2,1,256]{2,1,0:T(1,128)} %param.13) | data formatting | bytes 4096 | tf_op args[0]
  1.5 7.3 %all-to-all-start.2 = ((f32[2,1,256]{0,1,2:T(1,128)}), f32[2,1,256]{0,1,2:T(1,128)S(1)}, u32[]{:S(2)}, u32[]{:S(2)}) async-start(f32[2,1,256]{0,1,2:T(1,128)} %copy.39), calls=%async_computation.2 | async-start | bytes 262144 | tf_op jit(solution)/shard_map/all_to_all | solution.py:58
  8.8 1.5 %copy.35 = f32[2,1,256]{0,1,2:T(1,128)} copy(f32[2,1,256]{2,1,0:T(1,128)} %param.14) | data formatting | bytes 4096 | tf_op args[1]
  10.3 5.9 %all-to-all-done.2 = f32[2,1,256]{0,1,2:T(1,128)S(1)} async-done(((f32[2,1,256]{0,1,2:T(1,128)}), f32[2,1,256]{0,1,2:T(1,128)S(1)}, u32[]{:S(2)}, u32[]{:S(2)}) %all-to-all-start.2) | async-done | bytes 2080 | tf_op jit(solution)/shard_map/all_to_all | solution.py:58
  16.1 3.4 %all-to-all-start = ((f32[2,1,256]{0,1,2:T(1,128)}), f32[2,1,256]{0,1,2:T(1,128)S(1)}, u32[]{:S(2)}, u32[]{:S(2)}) async-start(f32[2,1,256]{0,1,2:T(1,128)} %copy.35), calls=%async_computation | async-start | bytes 262144 | tf_op jit(solution)/shard_map/all_to_all | solution.py:59
  19.5 0.7 %fusion.19 = s32[1,4,4,128]{3,2,1,0:T(4,128)S(1)} fusion(s32[4,512]{1,0:T(4,128)} %param.20), kind=kLoop, calls=%fused_computation.44 | loop fusion | flops 57344 | bytes 16384
  20.3 0.8 %copy.38 = f32[2,1,256]{0,1,2:T(1,128)S(1)} copy(f32[2,1,256]{2,1,0:T(1,128)} %param.15) | data formatting | bytes 4096 | tf_op args[2]
  21.1 0.8 %copy.37 = s32[2,256]{0,1:T(8,128)S(1)} copy(s32[2,256]{1,0:T(2,128)} %param.16) | data formatting | bytes 4096 | tf_op args[3]
  21.9 0.8 %mul.88 = f32[2,1,256]{0,1,2:T(1,128)} multiply(f32[2,1,256]{0,1,2:T(1,128)S(1)} %copy.38, f32[2,1,256]{0,1,2:T(1,128)S(1)} %bitcast.57) | non-fusion elementwise | flops 512 | bytes 6144 | tf_op jit(solution)/shard_map/mul | solution.py:44
  22.7 4.1 %all-to-all-done = f32[2,1,256]{0,1,2:T(1,128)S(1)} async-done(((f32[2,1,256]{0,1,2:T(1,128)}), f32[2,1,256]{0,1,2:T(1,128)S(1)}, u32[]{:S(2)}, u32[]{:S(2)}) %all-to-all-start) | async-done | bytes 2080 | tf_op jit(solution)/shard_map/all_to_all | solution.py:59
  26.8 3.4 %all-to-all-start.1 = ((f32[2,1,256]{0,1,2:T(1,128)}), f32[2,1,256]{0,1,2:T(1,128)S(1)}, u32[]{:S(2)}, u32[]{:S(2)}) async-start(f32[2,1,256]{0,1,2:T(1,128)} %mul.88), calls=%async_computation.1 | async-start | bytes 262144 | tf_op jit(solution)/shard_map/all_to_all | solution.py:60
  30.2 0.0 copy-done.2
  30.2 0.1 reshape.45
  30.3 0.0 copy-done.3
  30.3 0.1 reshape.43
  30.4 0.0 copy-done.1
  30.4 0.1 reshape.44
  30.5 0.2 copy.42
  30.7 0.1 copy.46
  30.8 0.1 copy.45
  30.9 6.6 %all-to-all-done.1 = f32[2,1,256]{0,1,2:T(1,128)S(1)} async-done(((f32[2,1,256]{0,1,2:T(1,128)}), f32[2,1,256]{0,1,2:T(1,128)S(1)}, u32[]{:S(2)}, u32[]{:S(2)}) %all-to-all-start.1) | async-done | bytes 2080 | tf_op jit(solution)/shard_map/all_to_all | solution.py:60
  37.5 0.1 copy.41
  37.6 13.1 %while.23 = (s32[]{:T(128)}, bf16[2,16,32]{2,1,0:T(8,128)(2,1)S(1)}, f32[2,8,32]{2,1,0:T(8,128)S(1)}, f32[2,8,32]{2,1,0:T(8,128)S(1)}, f32[2,8,32]{2,1,0:T(8,128...) while((s32[]{:T(128)}, ...), condition=%wide.region_5.6_spmd.clone, body=%wide.region_0.5_spmd.clone.sunk | while | flops 196900 | bytes 47346 | solution.py:64
  37.6 6.5 %while.24 = (s32[]{:T(128)}, bf16[16,32]{1,0:T(8,128)(2,1)S(1)}, f32[16,7]{1,0:T(8,128)S(1)}, f32[8,32]{1,0:T(8,128)S(1)}, f32[16,7,8]{2,1,0:T(8,128)S(1)}, /*in...) while((s32[]{:T(128)}, bf16[16,32]{1,0:T(8,128)(2,1)S(1)}, ...), condition=%wide.region_4.4_spmd, body=%wide.region_1.3_spmd.sunk | while | flops 196258 | bytes 32521 | solution.py:55
  37.7 0.3 multiply_add_fusion.3
  38.1 0.3 multiply_add_fusion.3
  38.5 0.3 multiply_add_fusion.3
  38.9 0.3 multiply_add_fusion.3
  39.3 0.3 multiply_add_fusion.3
  39.7 0.3 multiply_add_fusion.3
  40.1 0.3 multiply_add_fusion.3
  40.5 0.3 multiply_add_fusion.3
  40.9 0.3 multiply_add_fusion.3
  41.3 0.3 multiply_add_fusion.3
  41.7 0.3 multiply_add_fusion.3
  42.1 0.3 multiply_add_fusion.3
  42.5 0.3 multiply_add_fusion.3
  42.9 0.3 multiply_add_fusion.3
  43.3 0.3 multiply_add_fusion.3
  43.8 0.3 multiply_add_fusion.3
  44.2 6.5 %while.24 = (s32[]{:T(128)}, bf16[16,32]{1,0:T(8,128)(2,1)S(1)}, f32[16,7]{1,0:T(8,128)S(1)}, f32[8,32]{1,0:T(8,128)S(1)}, f32[16,7,8]{2,1,0:T(8,128)S(1)}, /*in...) while((s32[]{:T(128)}, bf16[16,32]{1,0:T(8,128)(2,1)S(1)}, ...), condition=%wide.region_4.4_spmd, body=%wide.region_1.3_spmd.sunk | while | flops 196258 | bytes 32521 | solution.py:55
  44.3 0.3 multiply_add_fusion.3
  44.7 0.3 multiply_add_fusion.3
  45.1 0.3 multiply_add_fusion.3
  45.5 0.3 multiply_add_fusion.3
  45.9 0.3 multiply_add_fusion.3
  46.3 0.3 multiply_add_fusion.3
  46.7 0.3 multiply_add_fusion.3
  47.1 0.3 multiply_add_fusion.3
  47.5 0.3 multiply_add_fusion.3
  47.9 0.3 multiply_add_fusion.3
  48.3 0.3 multiply_add_fusion.3
  48.7 0.3 multiply_add_fusion.3
  49.1 0.3 multiply_add_fusion.3
  49.5 0.3 multiply_add_fusion.3
  49.9 0.3 multiply_add_fusion.3
  50.3 0.3 multiply_add_fusion.3
  50.7 0.1 copy.43
  50.8 5.2 %all_gather.3 = bf16[2,16,128]{1,0,2:T(2,128)(2,1)S(1)} all-gather(bf16[2,16,32]{1,0,2:T(2,128)(2,1)S(1)} %copy.43), channel_id=1, replica_groups=mesh['slab'=8,'disk'=4] {'disk'}, dimensions={2}, use_global_device_ids=true | all-gather | bytes 10240 | tf_op jit(solution)/shard_map/all_gather | solution.py:67
  56.0 7.0 %gather_fusion = bf16[2048,2,16]{2,1,0:T(2,128)(2,1)S(1)} fusion(bf16[2,16,128]{1,0,2:T(2,128)(2,1)S(1)} %all_gather.3, s32[2048]{0:T(1024)S(1)} %broadcast_clamp_fusion), kind=kCustom, calls=%fused_computation | custom fusion | bytes 270336 | tf_op jit(solution)/shard_map/gather | solution.py:72
  63.1 0.0 copy-done
  63.1 6.1 %fusion.15 = f32[512,2,16]{2,1,0:T(2,128)S(1)} fusion(bf16[4,512,2,16]{3,2,1,0:T(2,128)(2,1)S(1)} %bitcast.56, f32[4,512]{1,0:T(4,128)S(1)} %copy-done), kind=kLoop, calls=%fused_computation.32 | loop fusion | flops 180224 | bytes 204800 | tf_op jit(solution)/shard_map/reduce_sum | solution.py:73
  69.2 0.8 %copy.44 = f32[2,16,512]{2,1,0:T(8,128)} copy(f32[2,16,512]{1,0,2:T(2,128)S(1)} %bitcast.55) | data formatting | bytes 131072 | tf_op jit(solution)/shard_map/reduce_sum | solution.py:73
  (209 shorter events, 3.6 us)
Async XLA Ops:
  0.0 30.2 %copy-start.2 = (f32[112]{0:T(128)S(1)}, f32[112]{0:T(128)}, u32[]{:S(2)}) copy-start(f32[112]{0:T(128)} %param.18) | copy-start | bytes 1348
  0.0 30.3 %copy-start.3 = (f32[112]{0:T(128)S(1)}, f32[112]{0:T(128)}, u32[]{:S(2)}) copy-start(f32[112]{0:T(128)} %param.19) | copy-start | bytes 1348
  0.0 30.4 %copy-start.1 = (f32[112,8]{0,1:T(8,128)S(1)}, f32[112,8]{0,1:T(8,128)}, u32[]{:S(2)}) copy-start(f32[112,8]{0,1:T(8,128)} %param.17) | copy-start | bytes 10756
  1.5 14.6 %all-to-all-start.2 = ((f32[2,1,256]{0,1,2:T(1,128)}), f32[2,1,256]{0,1,2:T(1,128)S(1)}, u32[]{:S(2)}, u32[]{:S(2)}) async-start(f32[2,1,256]{0,1,2:T(1,128)} %copy.39), calls=%async_computation.2 | async-start | bytes 262144 | tf_op jit(solution)/shard_map/all_to_all | solution.py:58
  16.1 10.7 %all-to-all-start = ((f32[2,1,256]{0,1,2:T(1,128)}), f32[2,1,256]{0,1,2:T(1,128)S(1)}, u32[]{:S(2)}, u32[]{:S(2)}) async-start(f32[2,1,256]{0,1,2:T(1,128)} %copy.35), calls=%async_computation | async-start | bytes 262144 | tf_op jit(solution)/shard_map/all_to_all | solution.py:59
  26.8 10.7 %all-to-all-start.1 = ((f32[2,1,256]{0,1,2:T(1,128)}), f32[2,1,256]{0,1,2:T(1,128)S(1)}, u32[]{:S(2)}, u32[]{:S(2)}) async-start(f32[2,1,256]{0,1,2:T(1,128)} %mul.88), calls=%async_computation.1 | async-start | bytes 262144 | tf_op jit(solution)/shard_map/all_to_all | solution.py:60
  37.6 25.5 %copy-start = (f32[4,512]{1,0:T(4,128)S(1)}, f32[4,512]{1,0:T(4,128)}, u32[]{:S(2)}) copy-start(f32[4,512]{1,0:T(4,128)} %param.21) | copy-start | bytes 24580
where the time goes:
time: 70.6 us; the launch traced here: 70 us
  waiting for transfers between devices  16.5 us (23%)
  local copies, waits for them, and re-layouts  15.3 us (22%)
  starting transfers between devices  14 us (20%)
  other arithmetic  9.16 us (13%)
  matrix products  8.2 us (12%)
  blocking collectives  5.25 us (7%)
  loops' own time  1.38 us (2%)
    dot_general x32, matrix products, band_block(): jnp.einsum('vh,qha->qva', upper_level_mask, optical_depth, precision=lax....  8.2 us
    all_to_all x1, starting transfers between devices, local(): lax.all_to_all(thermal_anomaly, 'slab', split_axis=2, concat_axis=1, tile...  7.28 us
    gather x1, local copies, waits for them, and re-layouts, local(): picked = strip_rad[:, :, strip_index].astype(jnp.float32)  7.05 us
    all_to_all x1, waiting for transfers between devices, local(): lax.all_to_all(overcast_fraction_intensity, 'slab', split_axis=2, concat_...  6.56 us
    reduce_sum x1, other arithmetic, local(): pixels = jnp.sum(picked * scene_interpolation_factors[None, None], axis=2)  6.07 us
    all_to_all x1, waiting for transfers between devices, local(): lax.all_to_all(thermal_anomaly, 'slab', split_axis=2, concat_axis=1, tile...  5.88 us
    all_gather x1, blocking collectives, local(): lax.all_gather(spectral_interval_intensity, 'disk', axis=2, tiled=True)  5.25 us
    unnamed x15, local copies, waits for them, and re-layouts  4.91 us
  transfers between devices with their start and end apart: 3, of which 3 were waited for; matrix products, arithmetic and copies ran while one was open for 8% of the time, Pallas kernels for 0%

commit v1 on v0

v1 whole, which is shorter than its diff:
```python
import functools

import jax
import jax.numpy as jnp
from jax import lax
from jax.experimental import pallas as pl
from jax.experimental.pallas import tpu as pltpu
from jax.sharding import PartitionSpec as P

BANDS = 16
GPB = 7
LANES = 128
MESH = pl.DeviceIdType.MESH
NEG_LOG2E = -1.4426950408889634


def loop(count, body):
    if count <= 64:
        for i in range(count):
            body(i)
    else:
        lax.fori_loop(0, count, lambda i, _: (body(i), 0)[1], 0)


def kernel(
    n_slab, n_disk, sector_cols, block_cols,
    t_hbm, q_hbm, c_hbm, o_hbm, mol_hbm, cond_hbm, pf_hbm, src_hbm, w_hbm,
    out_ref,
    t_ref, q_ref, c_ref, o_ref, mol_ref, cond_ref, pf_ref, src_ref, w_ref,
    fld, pk, recv, sel, mb, cb, pb, whi, wlo,
    in_sems, send_sem, recv_sem,
):
    n = n_slab * n_disk
    levels = n_slab
    halves = sector_cols // LANES
    per = LANES // block_cols
    me_s = lax.axis_index("slab")
    me_d = lax.axis_index("disk")
    me = me_s * n_disk + me_d

    ins = [
        pltpu.make_async_copy(a, b, in_sems.at[i])
        for i, (a, b) in enumerate(
            [(t_hbm, t_ref), (q_hbm, q_ref), (c_hbm, c_ref), (o_hbm, o_ref), (mol_hbm, mol_ref),
             (cond_hbm, cond_ref), (pf_hbm, pf_ref), (src_hbm, src_ref), (w_hbm, w_ref)]
        )
    ]
    for copy in ins:
        copy.start()

    barrier = pltpu.get_barrier_semaphore()

    def greet(i):
        peer = lax.rem(me + (i + 1), n)
        pl.semaphore_signal(
            barrier, inc=1, device_id=(peer // n_disk, lax.rem(peer, n_disk)), device_id_type=MESH
        )

    loop(n - 1, greet)

    for copy in ins[:4]:
        copy.wait()
    for h in range(2):
        for k in range(halves):
            cols = pl.ds(k * LANES, LANES)
            cloud = jnp.where(o_ref[h:h + 1, cols] == 1, c_ref[h, :, cols], 0.0)
            t2 = t_ref[h, :, cols] * t_ref[h, :, cols]
            fld[h, pl.ds(4 * k, 1), :] = t2 * t2
            fld[h, pl.ds(4 * k + 1, 1), :] = q_ref[h, :, cols]
            fld[h, pl.ds(4 * k + 2, 1), :] = cloud
            fld[h, pl.ds(4 * k + 3, 1), :] = cloud
    rows = 4 * halves
    lane = lax.broadcasted_iota(jnp.int32, (rows, LANES), 1)
    first_hour = (lane & block_cols) == 0
    turn = lax.rem(me_d, 2) * (2 * block_cols)
    f0 = fld[0]
    f1 = fld[1]
    for s in range(per):
        a = pltpu.roll(f0, lax.rem(turn + (LANES - s * block_cols), LANES), 1)
        b = pltpu.roll(f1, lax.rem(turn + (LANES + block_cols - s * block_cols), LANES), 1)
        p = jnp.where(first_hour, a, b)
        for k in range(halves):
            pk[k * per + s] = p[4 * k:4 * k + 4, :]

    pl.semaphore_wait(barrier, n - 1)

    def send(i):
        peer = lax.rem(me + (i + 1), n)
        ps = peer // n_disk
        pltpu.make_async_remote_copy(
            src_ref=pk.at[ps],
            dst_ref=recv.at[me],
            send_sem=send_sem,
            recv_sem=recv_sem,
            device_id=(ps, lax.rem(peer, n_disk)),
            device_id_type=MESH,
        ).start()

    loop(n - 1, send)
    recv[me] = pk[me_s]

    for copy in ins[4:]:
        copy.wait()
    g_lane = lax.broadcasted_iota(jnp.int32, (BANDS, BANDS * GPB), 1)
    g_band = lax.broadcasted_iota(jnp.int32, (BANDS, BANDS * GPB), 0)
    for j in range(GPB):
        m = mol_ref[pl.ds(j, BANDS, stride=GPB), :] * NEG_LOG2E
        for l in range(levels):
            mb[l, j] = jnp.broadcast_to(m[:, l:l + 1], (BANDS, LANES))
        hit = g_lane == g_band * GPB + j
        cv = jnp.sum(jnp.where(hit, cond_ref[...], 0.0), axis=1, keepdims=True) * NEG_LOG2E
        pv = jnp.sum(jnp.where(hit, pf_ref[...], 0.0), axis=1, keepdims=True)
        cb[j] = jnp.broadcast_to(cv, (BANDS, LANES))
        pb[j] = jnp.broadcast_to(pv, (BANDS, LANES))

    src = src_ref[...]
    place = lax.div(src, sector_cols) * block_cols + lax.rem(src, block_cols)
    w = w_ref[...]
    taps, pixels = w.shape
    row = lax.broadcasted_iota(jnp.int32, (block_cols, pixels), 0)
    for d in range(n_disk):
        acc = None
        for k in range(taps):
            term = jnp.where(row + d * block_cols == place[k:k + 1, :], w[k:k + 1, :], 0.0)
            acc = term if acc is None else acc + term
        hi = acc.astype(jnp.bfloat16)
        lo = (acc - hi.astype(jnp.float32)).astype(jnp.bfloat16)
        for h in range(2):
            at = pl.ds((2 * d + h) * block_cols, block_cols)
            whi[at, :] = hi
            wlo[at, :] = lo

    pltpu.make_async_remote_copy(
        src_ref=recv.at[pl.ds(0, n - 1)], dst_ref=recv.at[pl.ds(0, n - 1)],
        send_sem=send_sem, recv_sem=recv_sem, device_id=(me_s, me_d), device_id_type=MESH,
    ).wait_recv()

    left = lax.broadcasted_iota(jnp.int32, (4, LANES), 1) < 2 * block_cols
    lane16 = lax.broadcasted_iota(jnp.int32, (BANDS, LANES), 1)
    parts = []
    for pair in range(n_disk // 2):
        def fields(l):
            x = jnp.where(left, recv[l * n_disk + 2 * pair], recv[l * n_disk + 2 * pair + 1])
            return tuple(jnp.broadcast_to(x[f:f + 1, :], (8, LANES)) for f in range(3))

        if levels <= 8:
            held = [fields(l) for l in range(levels)]
        else:
            def fill(l):
                x = jnp.where(left, recv[l * n_disk + 2 * pair], recv[l * n_disk + 2 * pair + 1])
                sel[l] = x
            lax.fori_loop(0, levels, lambda l, _: (fill(l), 0)[1], 0)
        halves_out = []
        for half in range(BANDS // 8):
            at = pl.ds(8 * half, 8)
            total = None
            for j in range(GPB):
                cbj = cb[j, at, :]

                def step(l, carry):
                    depth, seen, emitted = carry
                    if levels <= 8:
                        b4, q, c = held[l]
                    else:
                        x = sel[l]
                        b4, q, c = x[0:1, :], x[1:2, :], x[2:3, :]
                    depth = depth + (mb[l, j, at, :] * q + cbj * c)
                    onward = jnp.exp2(depth)
                    emitted = emitted + b4 * (seen - onward)
                    return depth, onward, emitted

                zero = jnp.zeros((8, LANES), jnp.float32)
                carry = (zero, jnp.ones((8, LANES), jnp.float32), zero)
                if levels <= 8:
                    for l in range(levels):
                        carry = step(l, carry)
                    ground = held[levels - 1][0]
                else:
                    carry = lax.fori_loop(0, levels, step, carry)
                    ground = sel[levels - 1][0:1, :]
                got = pb[j, at, :] * (carry[2] + ground * carry[1])
                total = got if total is None else total + got
            halves_out.append(total)
        parts.append(jnp.concatenate(halves_out, axis=0) * (1.0 / GPB))

    hour = (lane16 & block_cols) != 0
    lhs = jnp.concatenate(
        [
            jnp.concatenate([jnp.where(hour == bool(h), r, 0.0) for r in parts], axis=1)
            for h in range(2)
        ],
        axis=0,
    ).astype(jnp.bfloat16)
    res = jnp.dot(lhs, whi[...], preferred_element_type=jnp.float32) + jnp.dot(
        lhs, wlo[...], preferred_element_type=jnp.float32
    )
    out_ref[0] = res[:BANDS]
    out_ref[1] = res[BANDS:]

    pltpu.make_async_remote_copy(
        src_ref=recv.at[pl.ds(0, n - 1)], dst_ref=recv.at[pl.ds(0, n - 1)],
        send_sem=send_sem, recv_sem=recv_sem, device_id=(me_s, me_d), device_id_type=MESH,
    ).wait_send()


def local(n_slab, n_disk, t, q, c, o, mol, cond, pf, src, w):
    hours, _, sector_cols = t.shape
    block_cols = sector_cols // n_slab
    taps, pixels = w.shape
    levels = mol.shape[1]
    n = n_slab * n_disk
    f32, bf16 = jnp.float32, jnp.bfloat16
    halves = sector_cols // LANES
    cond = cond.reshape(1, -1)
    pf = pf.reshape(1, -1)
    args = (t, q, c, o, mol, cond, pf, src, w)
    vmem = pltpu.VMEM
    return pl.pallas_call(
        functools.partial(kernel, n_slab, n_disk, sector_cols, block_cols),
        out_shape=jax.ShapeDtypeStruct((hours, BANDS, pixels), f32),
        in_specs=[pl.BlockSpec(memory_space=pl.ANY)] * len(args),
        out_specs=pl.BlockSpec(memory_space=pltpu.VMEM),
        scratch_shapes=[vmem(a.shape, a.dtype) for a in args]
        + [
            vmem((hours, 4 * halves, LANES), f32),
            vmem((n_slab, 4, LANES), f32),
            vmem((n, 4, LANES), f32),
            vmem((levels, 4, LANES), f32),
            vmem((levels, GPB, BANDS, LANES), f32),
            vmem((GPB, BANDS, LANES), f32),
            vmem((GPB, BANDS, LANES), f32),
            vmem((n_disk * 2 * block_cols, pixels), bf16),
            vmem((n_disk * 2 * block_cols, pixels), bf16),
            pltpu.SemaphoreType.DMA((len(args),)),
            pltpu.SemaphoreType.DMA,
            pltpu.SemaphoreType.DMA,
        ],
        compiler_params=pltpu.CompilerParams(
            collective_id=0, has_side_effects=True, vmem_limit_bytes=32 * 1024 * 1024
        ),
    )(*args)


def solution(mesh):
    in_specs = (
        P(None, "slab", "disk"),
        P(None, "slab", "disk"),
        P(None, "slab", "disk"),
        P(None, "disk"),
        P(),
        P(),
        P(),
        P(None, ("slab", "disk")),
        P(None, ("slab", "disk")),
    )
    out_specs = P(None, None, ("slab", "disk"))
    fn = functools.partial(local, mesh.shape["slab"], mesh.shape["disk"])
    return jax.shard_map(fn, mesh=mesh, in_specs=in_specs, out_specs=out_specs, check_vma=False)
```

time: 70.6 us -> 11.9 us (0.17)
  waiting for transfers between devices: 16.5 us -> 0 us
  starting transfers between devices: 14 us -> 0 us
  local copies, waits for them, and re-layouts: 15.3 us -> 1.53 us
  Pallas kernels: 0 us -> 10.1 us
  other arithmetic: 9.16 us -> 0 us
  matrix products: 8.2 us -> 0 us
  blocking collectives: 5.25 us -> 0 us
  loops' own time: 1.38 us -> 0 us
    all_to_all x3 -> x0, waiting for transfers between devices: 16.5 us -> none  [the longest x1 6.56 us: local(): lax.all_to_all(overcast_fraction_intensity, 'slab', split_axis=2, concat_...]
    all_to_all x3 -> x0, starting transfers between devices: 14 us -> none  [the longest x1 7.28 us: local(): lax.all_to_all(thermal_anomaly, 'slab', split_axis=2, concat_axis=1, tile...]
    pallas_call x0 -> x1, Pallas kernels: none -> 10.1 us  [local(): pl.pallas_call(functools.partial(kernel, n_slab, n_disk, sector_cols, blo...]
    dot_general x32 -> x0, matrix products: 8.2 us -> none  [band_block(): jnp.einsum('vh,qha->qva', upper_level_mask, optical_depth, precision=lax....]
    gather x1 -> x0, local copies, waits for them, and re-layouts: 7.05 us -> none  [local(): picked = strip_rad[:, :, strip_index].astype(jnp.float32)]
    reduce_sum x33 -> x0, other arithmetic: 6.72 us -> none  [the longest x1 6.07 us: local(): pixels = jnp.sum(picked * scene_interpolation_factors[None, None], axis=2)]
    all_gather x1 -> x0, blocking collectives: 5.25 us -> none  [local(): lax.all_gather(spectral_interval_intensity, 'disk', axis=2, tiled=True)]
    unnamed x15 -> x18, local copies, waits for them, and re-layouts: 4.91 us -> 1.53 us
  transfers between devices with their start and end apart: 3 -> 0, of which waited for: 3 -> 0; matrix products, arithmetic and copies ran while one was open for 8% -> 0% of each run, Pallas kernels for 0% -> 0%
where the time goes in v1:
time: 11.9 us; the launch traced here: 11.8 us
  Pallas kernels  10.1 us (85%)
  local copies, waits for them, and re-layouts  1.53 us (13%)
    pallas_call x1, Pallas kernels, local(): pl.pallas_call(functools.partial(kernel, n_slab, n_disk, sector_cols, blo...  10.1 us
    unnamed x18, local copies, waits for them, and re-layouts  1.53 us

profile of v1, /device:TPU:0, one launch (start us, length us, event | category | flops | bytes accessed | tf_op | source)
XLA Modules:
  0.0 11.8 jit_solution(2087129327795067249)
XLA Ops:
  0.0 0.0 copy-start
  0.0 0.0 copy-start.1
  0.0 0.0 copy-start.2
  0.0 0.0 copy-start.3
  0.0 0.0 copy-start.4
  0.0 0.0 copy-start.5
  0.0 0.0 copy-start.6
  0.0 0.0 copy-start.7
  0.0 0.9 %copy.10.mol_hbm = f32[112,8]{1,0:T(8,128)S(1)} copy(f32[112,8]{0,1:T(8,128)} %param.13) | data formatting | bytes 7168 | tf_op args[4]
  0.9 0.0 copy-done
  0.9 0.0 copy-done.1
  0.9 0.0 copy-done.2
  0.9 0.0 copy-done.3
  0.9 0.0 copy-done.4
  1.0 0.0 copy-done.5
  1.0 0.0 copy-done.6
  1.0 0.0 copy-done.7
  1.0 10.1 %shard_map.91 = f32[2,16,512]{2,1,0:T(8,128)S(1)} custom-call(f32[2,1,256]{2,1,0:T(1,128)S(1)} %copy-done.2, f32[2,1,256]{2,1,0:T(1,128)S(1)} %copy-done.3, f32[2,1,256]{2,1,0:T(1,128)S(1)} %copy-done.4, s32[2,256]{1,0:T(2,128)S(1)} %copy-done.5, f32[112,8]{1,0:T(8,128)S(1)} %copy.10.mol_hbm, f32[1,112]{1,0:T(1,128)S(1)} %bitcast.2, f32[1,112]{1,0:T(1,128)S(1)} %bitcast.3, ...), custom_call_target="tpu_custom_call" | custom-call | tf_op jit(solution)/shard_map/pallas_call | solution.py:218
  11.1 0.6 %copy.12 = f32[2,16,512]{2,1,0:T(8,128)} copy(f32[2,16,512]{2,1,0:T(8,128)S(1)} %shard_map.91) | data formatting | bytes 131072
Async XLA Ops:
  0.0 0.9 %copy-start = (s32[4,512]{1,0:T(4,128)S(1)}, s32[4,512]{1,0:T(4,128)}, u32[]{:S(2)}) copy-start(s32[4,512]{1,0:T(4,128)} %src_hbm.1) | copy-start | bytes 24580
  0.0 0.9 %copy-start.1 = (f32[4,512]{1,0:T(4,128)S(1)}, f32[4,512]{1,0:T(4,128)}, u32[]{:S(2)}) copy-start(f32[4,512]{1,0:T(4,128)} %w_hbm.1) | copy-start | bytes 24580
  0.0 0.9 %copy-start.2 = (f32[2,1,256]{2,1,0:T(1,128)S(1)}, f32[2,1,256]{2,1,0:T(1,128)}, u32[]{:S(2)}) copy-start(f32[2,1,256]{2,1,0:T(1,128)} %t_hbm.1) | copy-start | bytes 6148
  0.0 0.9 %copy-start.3 = (f32[2,1,256]{2,1,0:T(1,128)S(1)}, f32[2,1,256]{2,1,0:T(1,128)}, u32[]{:S(2)}) copy-start(f32[2,1,256]{2,1,0:T(1,128)} %q_hbm.1) | copy-start | bytes 6148
  0.0 0.9 %copy-start.4 = (f32[2,1,256]{2,1,0:T(1,128)S(1)}, f32[2,1,256]{2,1,0:T(1,128)}, u32[]{:S(2)}) copy-start(f32[2,1,256]{2,1,0:T(1,128)} %c_hbm.1) | copy-start | bytes 6148
  0.0 0.9 %copy-start.5 = (s32[2,256]{1,0:T(2,128)S(1)}, s32[2,256]{1,0:T(2,128)}, u32[]{:S(2)}) copy-start(s32[2,256]{1,0:T(2,128)} %o_hbm.1) | copy-start | bytes 6148
  0.0 0.9 %copy-start.6 = (f32[112]{0:T(128)S(1)}, f32[112]{0:T(128)}, u32[]{:S(2)}) copy-start(f32[112]{0:T(128)} %param.14) | copy-start | bytes 1348
  0.0 0.9 %copy-start.7 = (f32[112]{0:T(128)S(1)}, f32[112]{0:T(128)}, u32[]{:S(2)}) copy-start(f32[112]{0:T(128)} %param.15) | copy-start | bytes 1348

commit v2 on v1

--- a/solution.py
+++ b/solution.py
@@ -27,7 +27,7 @@
     t_hbm, q_hbm, c_hbm, o_hbm, mol_hbm, cond_hbm, pf_hbm, src_hbm, w_hbm,
     out_ref,
     t_ref, q_ref, c_ref, o_ref, mol_ref, cond_ref, pf_ref, src_ref, w_ref,
-    fld, pk, recv, sel, mb, cb, pb, whi, wlo,
+    fld, pk, recv, sel, cmat, ctr, mb, cb, pb, whi, wlo,
     in_sems, send_sem, recv_sem,
 ):
     n = n_slab * n_disk
@@ -45,7 +45,7 @@
              (cond_hbm, cond_ref), (pf_hbm, pf_ref), (src_hbm, src_ref), (w_hbm, w_ref)]
         )
     ]
-    for copy in ins:
+    for copy in ins[:4]:
         copy.start()
 
     barrier = pltpu.get_barrier_semaphore()
@@ -57,6 +57,8 @@
         )
 
     loop(n - 1, greet)
+    for copy in ins[4:]:
+        copy.start()
 
     for copy in ins[:4]:
         copy.wait()
@@ -101,17 +103,25 @@
 
     for copy in ins[4:]:
         copy.wait()
-    g_lane = lax.broadcasted_iota(jnp.int32, (BANDS, BANDS * GPB), 1)
-    g_band = lax.broadcasted_iota(jnp.int32, (BANDS, BANDS * GPB), 0)
+    gs = BANDS * GPB
+    cmat[...] = jnp.zeros_like(cmat)
+    cmat[pl.ds(0, levels), pl.ds(0, gs)] = mol_ref[...] * NEG_LOG2E
+    cmat[pl.ds(levels, 1), pl.ds(0, gs)] = cond_ref[...] * NEG_LOG2E
+    cmat[pl.ds(levels + 1, 1), pl.ds(0, gs)] = pf_ref[...]
+    blocks, _, width = ctr.shape
+    for k in range(blocks):
+        ctr[k] = jnp.transpose(cmat[pl.ds(k * width, width), :])
     for j in range(GPB):
-        m = mol_ref[pl.ds(j, BANDS, stride=GPB), :] * NEG_LOG2E
+        m = [ctr[k, pl.ds(j, BANDS, stride=GPB), :] for k in range(blocks)]
+
+        def column(l):
+            at = l % width
+            return jnp.broadcast_to(m[l // width][:, at:at + 1], (BANDS, LANES))
+
         for l in range(levels):
-            mb[l, j] = jnp.broadcast_to(m[:, l:l + 1], (BANDS, LANES))
-        hit = g_lane == g_band * GPB + j
-        cv = jnp.sum(jnp.where(hit, cond_ref[...], 0.0), axis=1, keepdims=True) * NEG_LOG2E
-        pv = jnp.sum(jnp.where(hit, pf_ref[...], 0.0), axis=1, keepdims=True)
-        cb[j] = jnp.broadcast_to(cv, (BANDS, LANES))
-        pb[j] = jnp.broadcast_to(pv, (BANDS, LANES))
+            mb[l, j] = column(l)
+        cb[j] = column(levels)
+        pb[j] = column(levels + 1)
 
     src = src_ref[...]
     place = lax.div(src, sector_cols) * block_cols + lax.rem(src, block_cols)
@@ -208,6 +218,9 @@
     block_cols = sector_cols // n_slab
     taps, pixels = w.shape
     levels = mol.shape[1]
+    mol = mol.T
+    blocks = pl.cdiv(levels + 8, LANES)
+    width = min(levels + 8, LANES)
     n = n_slab * n_disk
     f32, bf16 = jnp.float32, jnp.bfloat16
     halves = sector_cols // LANES
@@ -226,6 +239,8 @@
             vmem((n_slab, 4, LANES), f32),
             vmem((n, 4, LANES), f32),
             vmem((levels, 4, LANES), f32),
+            vmem((blocks * width, LANES), f32),
+            vmem((blocks, LANES, width), f32),
             vmem((levels, GPB, BANDS, LANES), f32),
             vmem((GPB, BANDS, LANES), f32),
             vmem((GPB, BANDS, LANES), f32),
@@ -236,7 +251,7 @@
             pltpu.SemaphoreType.DMA,
         ],
         compiler_params=pltpu.CompilerParams(
-            collective_id=0, has_side_effects=True, vmem_limit_bytes=32 * 1024 * 1024
+            collective_id=0, has_side_effects=True, vmem_limit_bytes=60 * 1024 * 1024
         ),
     )(*args)
 

time: 11.9 us -> 12.3 us (1.034)
  Pallas kernels: 10.1 us -> 10.7 us
    pallas_call x1, Pallas kernels: 10.1 us -> 10.7 us  [local(): pl.pallas_call(functools.partial(kernel, n_slab, n_disk, sector_cols, blo...]
    unnamed x18 -> x1, local copies, waits for them, and re-layouts: 1.53 us -> 1.47 us
where the time goes in v2:
time: 12.3 us; the launch traced here: 12.2 us
  Pallas kernels  10.7 us (87%)
  local copies, waits for them, and re-layouts  1.47 us (12%)
    pallas_call x1, Pallas kernels, local(): pl.pallas_call(functools.partial(kernel, n_slab, n_disk, sector_cols, blo...  10.7 us
    unnamed x1, local copies, waits for them, and re-layouts  1.47 us

profile of v2, /device:TPU:0, one launch (start us, length us, event | category | flops | bytes accessed | tf_op | source)
XLA Modules:
  0.0 12.2 jit_solution(9861320560968469220)
XLA Ops:
  0.0 10.7 %shard_map.91 = f32[2,16,512]{2,1,0:T(8,128)} custom-call(f32[2,1,256]{2,1,0:T(1,128)} %t_hbm.1, f32[2,1,256]{2,1,0:T(1,128)} %q_hbm.1, f32[2,1,256]{2,1,0:T(1,128)} %c_hbm.1, s32[2,256]{1,0:T(2,128)} %o_hbm.1, f32[8,112]{1,0:T(8,128)} %bitcast.3, f32[1,112]{1,0:T(1,128)} %bitcast.4, f32[1,112]{1,0:T(1,128)} %bitcast.5, s32[4,512]{1,0:T(4,128)} %src_hbm.1, ...), custom_call_target="tpu_custom_call" | custom-call | tf_op jit(solution)/shard_map/pallas_call | solution.py:231
  10.7 1.5 %copy.11 = f32[2,16,512]{2,1,0:T(8,128)} copy(f32[2,16,512]{2,1,0:T(8,128)} %shard_map.91) | data formatting | bytes 131072

commit v3 on v1

v3 whole, which is shorter than its diff:
```python
import functools

import jax
import jax.numpy as jnp
from jax import lax
from jax.experimental import pallas as pl
from jax.experimental.pallas import tpu as pltpu
from jax.sharding import PartitionSpec as P

BANDS = 16
GPB = 7
LANES = 128
MESH = pl.DeviceIdType.MESH
NEG_LOG2E = -1.4426950408889634


def split(x):
    hi = x.astype(jnp.bfloat16).astype(jnp.float32)
    return hi, x - hi


def div(x, by):
    return x >> (by.bit_length() - 1) if by & (by - 1) == 0 else lax.div(x, by)


def rem(x, by):
    return x & (by - 1) if by & (by - 1) == 0 else lax.rem(x, by)


def kernel(
    n_slab, n_disk, sector_cols, block_cols,
    t_ref, q_ref, c_ref, o_ref, mol_ref, cond_ref, pf_ref, src_ref, w_ref,
    out_ref,
    fld, pk, recv, cmat, mmat, amat, fmat, bmat, smat, whi, wlo,
    send_sem, recv_sem,
):
    n = n_slab * n_disk
    levels = n_slab
    gs = BANDS * GPB
    halves = sector_cols // LANES
    per = LANES // block_cols
    me_s = lax.axis_index("slab")
    me_d = lax.axis_index("disk")
    me = me_s * n_disk + me_d

    barrier = pltpu.get_barrier_semaphore()

    def greet(i, carry):
        peer = rem(me + (i + 1), n)
        pl.semaphore_signal(
            barrier, inc=1, device_id=(div(peer, n_disk), rem(peer, n_disk)), device_id_type=MESH
        )
        return carry

    lax.fori_loop(0, n - 1, greet, 0)

    for h in range(2):
        for k in range(halves):
            cols = pl.ds(k * LANES, LANES)
            cloud = jnp.where(o_ref[h:h + 1, cols] == 1, c_ref[h, :, cols], 0.0)
            t2 = t_ref[h, :, cols] * t_ref[h, :, cols]
            fld[h, pl.ds(4 * k, 1), :] = t2 * t2
            fld[h, pl.ds(4 * k + 1, 1), :] = q_ref[h, :, cols]
            fld[h, pl.ds(4 * k + 2, 1), :] = cloud
            fld[h, pl.ds(4 * k + 3, 1), :] = cloud
    rows = 4 * halves
    lane = lax.broadcasted_iota(jnp.int32, (rows, LANES), 1)
    first_hour = (lane & block_cols) == 0
    turn = rem(me_d, 2) * (2 * block_cols)
    f0 = pltpu.roll(fld[0], turn, 1)
    f1 = pltpu.roll(fld[1], turn, 1)
    for s in range(per):
        x = pltpu.roll(f0, (LANES - s * block_cols) % LANES, 1) if s else f0
        y = pltpu.roll(f1, (LANES + block_cols - s * block_cols) % LANES, 1) if s != 1 else f1
        p = jnp.where(first_hour, x, y)
        for k in range(halves):
            pk[k * per + s] = p[4 * k:4 * k + 4, :]

    pl.semaphore_wait(barrier, n - 1)

    def send(i, carry):
        peer = rem(me + (i + 1), n)
        ps = div(peer, n_disk)
        pltpu.make_async_remote_copy(
            src_ref=pk.at[ps],
            dst_ref=recv.at[me],
            send_sem=send_sem,
            recv_sem=recv_sem,
            device_id=(ps, rem(peer, n_disk)),
            device_id_type=MESH,
        ).start()
        return carry

    lax.fori_loop(0, n - 1, send, 0)
    recv[me] = pk[me_s]

    mol_hi, mol_lo = split(jnp.transpose(mol_ref[...]) * NEG_LOG2E)
    cond_hi, cond_lo = split(cond_ref[...] * NEG_LOG2E)
    cmat[...] = jnp.zeros_like(cmat)
    for at, part in enumerate((mol_hi, cond_hi, mol_lo, cond_lo, mol_hi, cond_hi)):
        cmat[pl.ds(at * levels, levels), pl.ds(0, gs)] = jnp.broadcast_to(part, (levels, gs))
    mmat[...] = jnp.transpose(cmat[...])
    col = rem(lax.broadcasted_iota(jnp.int32, (gs, 6 * levels), 1), levels)

    def upto(l):
        return jnp.where(col <= l, mmat[pl.ds(0, gs), :], 0.0).astype(jnp.bfloat16)

    if levels <= 8:
        for l in range(levels):
            amat[l] = upto(l)

    g_lane = lax.broadcasted_iota(jnp.int32, (BANDS, gs), 1)
    g_band = lax.broadcasted_iota(jnp.int32, (BANDS, gs), 0) * GPB
    inside = (g_lane >= g_band) & (g_lane < g_band + GPB)
    s_hi, s_lo = split(jnp.where(inside, pf_ref[...] * (1.0 / GPB), 0.0))
    smat[pl.ds(0, BANDS), :] = s_hi.astype(jnp.bfloat16)
    smat[pl.ds(BANDS, BANDS), :] = s_lo.astype(jnp.bfloat16)

    src = src_ref[...]
    place = div(src, sector_cols) * block_cols + rem(src, block_cols)
    w = w_ref[...]
    taps, pixels = w.shape
    row = lax.broadcasted_iota(jnp.int32, (block_cols, pixels), 0)
    for d in range(n_disk):
        acc = None
        for k in range(taps):
            term = jnp.where(row + d * block_cols == place[k:k + 1, :], w[k:k + 1, :], 0.0)
            acc = term if acc is None else acc + term
        hi, lo = split(acc)
        hi = hi.astype(jnp.bfloat16)
        lo = lo.astype(jnp.bfloat16)
        for h in range(2):
            at = pl.ds((2 * d + h) * block_cols, block_cols)
            whi[at, :] = hi
            wlo[at, :] = lo

    arrive = pltpu.make_async_remote_copy(
        src_ref=recv.at[pl.ds(0, n - 1)], dst_ref=recv.at[pl.ds(0, n - 1)],
        send_sem=send_sem, recv_sem=recv_sem, device_id=(me_s, me_d), device_id_type=MESH,
    )
    arrive.wait_recv()

    left = lax.broadcasted_iota(jnp.int32, (4, LANES), 1) < 2 * block_cols
    for pair in range(n_disk // 2):
        cols = pl.ds(pair * LANES, LANES)

        def place_level(l, cols=cols, pair=pair):
            x = jnp.where(left, recv[l * n_disk + 2 * pair], recv[l * n_disk + 2 * pair + 1])
            bmat[pl.ds(l, 1), cols] = x[0:1, :]
            fmat[pl.ds(l, 1), cols] = x[1:2, :]
            fmat[pl.ds(levels + l, 1), cols] = x[2:3, :]

        for l in range(levels):
            place_level(l)
    f_hi, f_lo = split(fmat[...])
    fields = jnp.concatenate([f_hi, f_hi, f_lo], axis=0).astype(jnp.bfloat16)

    def step(l, a, carry):
        seen, emitted = carry
        onward = jnp.exp2(jnp.dot(a, fields, preferred_element_type=jnp.float32))
        return onward, emitted + bmat[pl.ds(l, 1), :] * (seen - onward)

    shape = (gs, fields.shape[1])
    carry = (jnp.ones(shape, jnp.float32), jnp.zeros(shape, jnp.float32))
    if levels <= 8:
        for l in range(levels):
            carry = step(l, amat[l], carry)
    else:
        carry = lax.fori_loop(0, levels, lambda l, c: step(l, upto(l), c), carry)
    e_hi, e_lo = split(carry[1] + bmat[pl.ds(levels - 1, 1), :] * carry[0])
    both = jnp.dot(smat[...], e_hi.astype(jnp.bfloat16), preferred_element_type=jnp.float32)
    rad = both[:BANDS] + both[BANDS:] + jnp.dot(
        smat[pl.ds(0, BANDS), :], e_lo.astype(jnp.bfloat16), preferred_element_type=jnp.float32
    )

    hour = (lax.broadcasted_iota(jnp.int32, rad.shape, 1) & block_cols) != 0
    lhs = jnp.concatenate([jnp.where(hour, 0.0, rad), jnp.where(hour, rad, 0.0)], axis=0)
    lhs = lhs.astype(jnp.bfloat16)
    res = jnp.dot(lhs, whi[...], preferred_element_type=jnp.float32) + jnp.dot(
        lhs, wlo[...], preferred_element_type=jnp.float32
    )
    out_ref[0] = res[:BANDS]
    out_ref[1] = res[BANDS:]
    arrive.wait_send()


def local(n_slab, n_disk, t, q, c, o, mol, cond, pf, src, w):
    hours, _, sector_cols = t.shape
    block_cols = sector_cols // n_slab
    taps, pixels = w.shape
    levels = mol.shape[1]
    n = n_slab * n_disk
    f32, bf16 = jnp.float32, jnp.bfloat16
    halves = sector_cols // LANES
    assert hours == 2 and n_disk * block_cols == LANES and n_disk == 4
    cond = cond.reshape(1, -1)
    pf = pf.reshape(1, -1)
    gs = BANDS * GPB
    kept = levels if levels <= 8 else 1
    args = (t, q, c, o, mol, cond, pf, src, w)
    vmem = pltpu.VMEM
    return pl.pallas_call(
        functools.partial(kernel, n_slab, n_disk, sector_cols, block_cols),
        out_shape=jax.ShapeDtypeStruct((hours, BANDS, pixels), f32),
        in_specs=[pl.BlockSpec(memory_space=pltpu.VMEM)] * len(args),
        out_specs=pl.BlockSpec(memory_space=pltpu.VMEM),
        scratch_shapes=[
            vmem((hours, 4 * halves, LANES), f32),
            vmem((n_slab, 4, LANES), f32),
            vmem((n, 4, LANES), f32),
            vmem((6 * levels, LANES), f32),
            vmem((LANES, 6 * levels), f32),
            vmem((kept, gs, 6 * levels), bf16),
            vmem((2 * levels, 2 * LANES), f32),
            vmem((levels, 2 * LANES), f32),
            vmem((2 * BANDS, gs), bf16),
            vmem((2 * LANES, pixels), bf16),
            vmem((2 * LANES, pixels), bf16),
            pltpu.SemaphoreType.DMA,
            pltpu.SemaphoreType.DMA,
        ],
        compiler_params=pltpu.CompilerParams(
            collective_id=0, has_side_effects=True, vmem_limit_bytes=32 * 1024 * 1024
        ),
    )(*args)


def solution(mesh):
    in_specs = (
        P(None, "slab", "disk"),
        P(None, "slab", "disk"),
        P(None, "slab", "disk"),
        P(None, "disk"),
        P(),
        P(),
        P(),
        P(None, ("slab", "disk")),
        P(None, ("slab", "disk")),
    )
    out_specs = P(None, None, ("slab", "disk"))
    fn = functools.partial(local, mesh.shape["slab"], mesh.shape["disk"])
    return jax.shard_map(fn, mesh=mesh, in_specs=in_specs, out_specs=out_specs, check_vma=False)
```

time: 11.9 us -> 11.9 us (level)
  no operation moved by 1% of the time
where the time goes in v3:
time: 11.9 us; the launch traced here: 11.8 us
  Pallas kernels  10.2 us (86%)
  local copies, waits for them, and re-layouts  1.53 us (13%)
    pallas_call x1, Pallas kernels, local(): pl.pallas_call(functools.partial(kernel, n_slab, n_disk, sector_cols, blo...  10.2 us
    unnamed x18, local copies, waits for them, and re-layouts  1.53 us

profile of v3, /device:TPU:0, one launch (start us, length us, event | category | flops | bytes accessed | tf_op | source)
XLA Modules:
  0.0 11.8 jit_solution(8797432930401045105)
XLA Ops:
  0.0 0.0 copy-start
  0.0 0.0 copy-start.1
  0.0 0.0 copy-start.2
  0.0 0.0 copy-start.3
  0.0 0.0 copy-start.4
  0.0 0.0 copy-start.5
  0.0 0.0 copy-start.6
  0.0 0.0 copy-start.7
  0.0 0.9 %copy.10.mol_ref = f32[112,8]{1,0:T(8,128)S(1)} copy(f32[112,8]{0,1:T(8,128)} %param.13) | data formatting | bytes 7168 | tf_op args[4]
  0.9 0.0 copy-done
  0.9 0.0 copy-done.1
  0.9 0.0 copy-done.2
  0.9 0.0 copy-done.3
  0.9 0.0 copy-done.4
  1.0 0.0 copy-done.5
  1.0 0.0 copy-done.6
  1.0 0.0 copy-done.7
  1.0 10.2 %shard_map.91 = f32[2,16,512]{2,1,0:T(8,128)S(1)} custom-call(f32[2,1,256]{2,1,0:T(1,128)S(1)} %copy-done.2, f32[2,1,256]{2,1,0:T(1,128)S(1)} %copy-done.3, f32[2,1,256]{2,1,0:T(1,128)S(1)} %copy-done.4, s32[2,256]{1,0:T(2,128)S(1)} %copy-done.5, f32[112,8]{1,0:T(8,128)S(1)} %copy.10.mol_ref, f32[1,112]{1,0:T(1,128)S(1)} %bitcast.2, f32[1,112]{1,0:T(1,128)S(1)} %bitcast.3, ...), custom_call_target="tpu_custom_call" | custom-call | tf_op jit(solution)/shard_map/pallas_call | solution.py:202
  11.1 0.6 %copy.12 = f32[2,16,512]{2,1,0:T(8,128)} copy(f32[2,16,512]{2,1,0:T(8,128)S(1)} %shard_map.91) | data formatting | bytes 131072
Async XLA Ops:
  0.0 0.9 %copy-start = (s32[4,512]{1,0:T(4,128)S(1)}, s32[4,512]{1,0:T(4,128)}, u32[]{:S(2)}) copy-start(s32[4,512]{1,0:T(4,128)} %src_ref.1) | copy-start | bytes 24580
  0.0 0.9 %copy-start.1 = (f32[4,512]{1,0:T(4,128)S(1)}, f32[4,512]{1,0:T(4,128)}, u32[]{:S(2)}) copy-start(f32[4,512]{1,0:T(4,128)} %w_ref.1) | copy-start | bytes 24580
  0.0 0.9 %copy-start.2 = (f32[2,1,256]{2,1,0:T(1,128)S(1)}, f32[2,1,256]{2,1,0:T(1,128)}, u32[]{:S(2)}) copy-start(f32[2,1,256]{2,1,0:T(1,128)} %t_ref.1) | copy-start | bytes 6148
  0.0 0.9 %copy-start.3 = (f32[2,1,256]{2,1,0:T(1,128)S(1)}, f32[2,1,256]{2,1,0:T(1,128)}, u32[]{:S(2)}) copy-start(f32[2,1,256]{2,1,0:T(1,128)} %q_ref.1) | copy-start | bytes 6148
  0.0 0.9 %copy-start.4 = (f32[2,1,256]{2,1,0:T(1,128)S(1)}, f32[2,1,256]{2,1,0:T(1,128)}, u32[]{:S(2)}) copy-start(f32[2,1,256]{2,1,0:T(1,128)} %c_ref.1) | copy-start | bytes 6148
  0.0 0.9 %copy-start.5 = (s32[2,256]{1,0:T(2,128)S(1)}, s32[2,256]{1,0:T(2,128)}, u32[]{:S(2)}) copy-start(s32[2,256]{1,0:T(2,128)} %o_ref.1) | copy-start | bytes 6148
  0.0 0.9 %copy-start.6 = (f32[112]{0:T(128)S(1)}, f32[112]{0:T(128)}, u32[]{:S(2)}) copy-start(f32[112]{0:T(128)} %param.14) | copy-start | bytes 1348
  0.0 0.9 %copy-start.7 = (f32[112]{0:T(128)S(1)}, f32[112]{0:T(128)}, u32[]{:S(2)}) copy-start(f32[112]{0:T(128)} %param.15) | copy-start | bytes 1348

commit v4 on v3

--- a/solution.py
+++ b/solution.py
@@ -14,6 +14,14 @@
 NEG_LOG2E = -1.4426950408889634
 
 
+def loop(count, body):
+    if count <= 64:
+        for i in range(count):
+            body(i)
+    else:
+        lax.fori_loop(0, count, lambda i, _: (body(i), 0)[1], 0)
+
+
 def split(x):
     hi = x.astype(jnp.bfloat16).astype(jnp.float32)
     return hi, x - hi
@@ -31,28 +39,32 @@
     n_slab, n_disk, sector_cols, block_cols,
     t_ref, q_ref, c_ref, o_ref, mol_ref, cond_ref, pf_ref, src_ref, w_ref,
     out_ref,
-    fld, pk, recv, cmat, mmat, amat, fmat, bmat, smat, whi, wlo,
-    send_sem, recv_sem,
+    fld, pk, recv, radb, cmat, mmat, amat, fmat, bmat, smat, whi, wlo,
+    send_sem, recv_sem, rad_send, rad_recv,
 ):
-    n = n_slab * n_disk
     levels = n_slab
     gs = BANDS * GPB
     halves = sector_cols // LANES
     per = LANES // block_cols
     me_s = lax.axis_index("slab")
     me_d = lax.axis_index("disk")
-    me = me_s * n_disk + me_d
+
+    def slab_peer(i):
+        return rem(me_s + (i + 1), n_slab)
+
+    def disk_peer(i):
+        return rem(me_d + (i + 1), n_disk)
 
     barrier = pltpu.get_barrier_semaphore()
 
-    def greet(i, carry):
-        peer = rem(me + (i + 1), n)
-        pl.semaphore_signal(
-            barrier, inc=1, device_id=(div(peer, n_disk), rem(peer, n_disk)), device_id_type=MESH
-        )
-        return carry
-
-    lax.fori_loop(0, n - 1, greet, 0)
+    def greet_slab(i):
+        pl.semaphore_signal(barrier, inc=1, device_id=(slab_peer(i), me_d), device_id_type=MESH)
+
+    def greet_disk(i):
+        pl.semaphore_signal(barrier, inc=1, device_id=(me_s, disk_peer(i)), device_id_type=MESH)
+
+    loop(n_slab - 1, greet_slab)
+    loop(n_disk - 1, greet_disk)
 
     for h in range(2):
         for k in range(halves):
@@ -76,23 +88,21 @@
         for k in range(halves):
             pk[k * per + s] = p[4 * k:4 * k + 4, :]
 
-    pl.semaphore_wait(barrier, n - 1)
-
-    def send(i, carry):
-        peer = rem(me + (i + 1), n)
-        ps = div(peer, n_disk)
+    pl.semaphore_wait(barrier, n_slab + n_disk - 2)
+
+    def send(i):
+        peer = slab_peer(i)
         pltpu.make_async_remote_copy(
-            src_ref=pk.at[ps],
-            dst_ref=recv.at[me],
+            src_ref=pk.at[peer],
+            dst_ref=recv.at[me_s],
             send_sem=send_sem,
             recv_sem=recv_sem,
-            device_id=(ps, rem(peer, n_disk)),
+            device_id=(peer, me_d),
             device_id_type=MESH,
         ).start()
-        return carry
-
-    lax.fori_loop(0, n - 1, send, 0)
-    recv[me] = pk[me_s]
+
+    loop(n_slab - 1, send)
+    recv[me_s] = pk[me_s]
 
     mol_hi, mol_lo = split(jnp.transpose(mol_ref[...]) * NEG_LOG2E)
     cond_hi, cond_lo = split(cond_ref[...] * NEG_LOG2E)
@@ -115,6 +125,52 @@
     s_hi, s_lo = split(jnp.where(inside, pf_ref[...] * (1.0 / GPB), 0.0))
     smat[pl.ds(0, BANDS), :] = s_hi.astype(jnp.bfloat16)
     smat[pl.ds(BANDS, BANDS), :] = s_lo.astype(jnp.bfloat16)
+
+    arrive = pltpu.make_async_remote_copy(
+        src_ref=recv.at[pl.ds(0, n_slab - 1)], dst_ref=recv.at[pl.ds(0, n_slab - 1)],
+        send_sem=send_sem, recv_sem=recv_sem, device_id=(me_s, me_d), device_id_type=MESH,
+    )
+    arrive.wait_recv()
+
+    for l in range(levels):
+        x = recv[l]
+        bmat[pl.ds(l, 1), :] = x[0:1, :]
+        fmat[pl.ds(l, 1), :] = x[1:2, :]
+        fmat[pl.ds(levels + l, 1), :] = x[2:3, :]
+    f_hi, f_lo = split(fmat[...])
+    fields = jnp.concatenate([f_hi, f_hi, f_lo], axis=0).astype(jnp.bfloat16)
+
+    def step(l, a, carry):
+        seen, emitted = carry
+        onward = jnp.exp2(jnp.dot(a, fields, preferred_element_type=jnp.float32))
+        return onward, emitted + bmat[pl.ds(l, 1), :] * (seen - onward)
+
+    shape = (gs, fields.shape[1])
+    carry = (jnp.ones(shape, jnp.float32), jnp.zeros(shape, jnp.float32))
+    if levels <= 8:
+        for l in range(levels):
+            carry = step(l, amat[l], carry)
+    else:
+        carry = lax.fori_loop(0, levels, lambda l, c: step(l, upto(l), c), carry)
+    e_hi, e_lo = split(carry[1] + bmat[pl.ds(levels - 1, 1), :] * carry[0])
+    both = jnp.dot(smat[...], e_hi.astype(jnp.bfloat16), preferred_element_type=jnp.float32)
+    mine = both[:BANDS] + both[BANDS:] + jnp.dot(
+        smat[pl.ds(0, BANDS), :], e_lo.astype(jnp.bfloat16), preferred_element_type=jnp.float32
+    )
+
+    radb[me_d] = mine.astype(jnp.bfloat16)
+
+    def share(i):
+        pltpu.make_async_remote_copy(
+            src_ref=radb.at[me_d],
+            dst_ref=radb.at[me_d],
+            send_sem=rad_send,
+            recv_sem=rad_recv,
+            device_id=(me_s, disk_peer(i)),
+            device_id_type=MESH,
+        ).start()
+
+    loop(n_disk - 1, share)
 
     src = src_ref[...]
     place = div(src, sector_cols) * block_cols + rem(src, block_cols)
@@ -134,45 +190,22 @@
             whi[at, :] = hi
             wlo[at, :] = lo
 
-    arrive = pltpu.make_async_remote_copy(
-        src_ref=recv.at[pl.ds(0, n - 1)], dst_ref=recv.at[pl.ds(0, n - 1)],
-        send_sem=send_sem, recv_sem=recv_sem, device_id=(me_s, me_d), device_id_type=MESH,
-    )
-    arrive.wait_recv()
-
-    left = lax.broadcasted_iota(jnp.int32, (4, LANES), 1) < 2 * block_cols
-    for pair in range(n_disk // 2):
-        cols = pl.ds(pair * LANES, LANES)
-
-        def place_level(l, cols=cols, pair=pair):
-            x = jnp.where(left, recv[l * n_disk + 2 * pair], recv[l * n_disk + 2 * pair + 1])
-            bmat[pl.ds(l, 1), cols] = x[0:1, :]
-            fmat[pl.ds(l, 1), cols] = x[1:2, :]
-            fmat[pl.ds(levels + l, 1), cols] = x[2:3, :]
-
-        for l in range(levels):
-            place_level(l)
-    f_hi, f_lo = split(fmat[...])
-    fields = jnp.concatenate([f_hi, f_hi, f_lo], axis=0).astype(jnp.bfloat16)
-
-    def step(l, a, carry):
-        seen, emitted = carry
-        onward = jnp.exp2(jnp.dot(a, fields, preferred_element_type=jnp.float32))
-        return onward, emitted + bmat[pl.ds(l, 1), :] * (seen - onward)
-
-    shape = (gs, fields.shape[1])
-    carry = (jnp.ones(shape, jnp.float32), jnp.zeros(shape, jnp.float32))
-    if levels <= 8:
-        for l in range(levels):
-            carry = step(l, amat[l], carry)
-    else:
-        carry = lax.fori_loop(0, levels, lambda l, c: step(l, upto(l), c), carry)
-    e_hi, e_lo = split(carry[1] + bmat[pl.ds(levels - 1, 1), :] * carry[0])
-    both = jnp.dot(smat[...], e_hi.astype(jnp.bfloat16), preferred_element_type=jnp.float32)
-    rad = both[:BANDS] + both[BANDS:] + jnp.dot(
-        smat[pl.ds(0, BANDS), :], e_lo.astype(jnp.bfloat16), preferred_element_type=jnp.float32
-    )
-
+    shared = pltpu.make_async_remote_copy(
+        src_ref=radb.at[pl.ds(0, n_disk - 1)], dst_ref=radb.at[pl.ds(0, n_disk - 1)],
+        send_sem=rad_send, recv_sem=rad_recv, device_id=(me_s, me_d), device_id_type=MESH,
+    )
+    shared.wait_recv()
+    lane_out = lax.broadcasted_iota(jnp.int32, (BANDS, LANES), 1)
+    left = lane_out < 2 * block_cols
+    rad = jnp.concatenate(
+        [
+            jnp.where(
+                left, radb[2 * pair].astype(jnp.float32), radb[2 * pair + 1].astype(jnp.float32)
+            )
+            for pair in range(n_disk // 2)
+        ],
+        axis=1,
+    )
     hour = (lax.broadcasted_iota(jnp.int32, rad.shape, 1) & block_cols) != 0
     lhs = jnp.concatenate([jnp.where(hour, 0.0, rad), jnp.where(hour, rad, 0.0)], axis=0)
     lhs = lhs.astype(jnp.bfloat16)
@@ -182,6 +215,7 @@
     out_ref[0] = res[:BANDS]
     out_ref[1] = res[BANDS:]
     arrive.wait_send()
+    shared.wait_send()
 
 
 def local(n_slab, n_disk, t, q, c, o, mol, cond, pf, src, w):
@@ -189,7 +223,6 @@
     block_cols = sector_cols // n_slab
     taps, pixels = w.shape
     levels = mol.shape[1]
-    n = n_slab * n_disk
     f32, bf16 = jnp.float32, jnp.bfloat16
     halves = sector_cols // LANES
     assert hours == 2 and n_disk * block_cols == LANES and n_disk == 4
@@ -207,15 +240,18 @@
         scratch_shapes=[
             vmem((hours, 4 * halves, LANES), f32),
             vmem((n_slab, 4, LANES), f32),
-            vmem((n, 4, LANES), f32),
+            vmem((n_slab, 4, LANES), f32),
+            vmem((n_disk, BANDS, LANES), bf16),
             vmem((6 * levels, LANES), f32),
             vmem((LANES, 6 * levels), f32),
             vmem((kept, gs, 6 * levels), bf16),
-            vmem((2 * levels, 2 * LANES), f32),
-            vmem((levels, 2 * LANES), f32),
+            vmem((2 * levels, LANES), f32),
+            vmem((levels, LANES), f32),
             vmem((2 * BANDS, gs), bf16),
             vmem((2 * LANES, pixels), bf16),
             vmem((2 * LANES, pixels), bf16),
+            pltpu.SemaphoreType.DMA,
+            pltpu.SemaphoreType.DMA,
             pltpu.SemaphoreType.DMA,
             pltpu.SemaphoreType.DMA,
         ],

time: 11.9 us -> 13.7 us (1.15)
  Pallas kernels: 10.2 us -> 12 us
    pallas_call x1, Pallas kernels: 10.2 us -> 12 us  [local(): pl.pallas_call(functools.partial(kernel, n_slab, n_disk, sector_cols, blo...]
where the time goes in v4:
time: 13.7 us; the launch traced here: 13.6 us
  Pallas kernels  12 us (88%)
  local copies, waits for them, and re-layouts  1.53 us (11%)
    pallas_call x1, Pallas kernels, local(): pl.pallas_call(functools.partial(kernel, n_slab, n_disk, sector_cols, blo...  12 us
    unnamed x18, local copies, waits for them, and re-layouts  1.53 us

profile of v4, /device:TPU:0, one launch (start us, length us, event | category | flops | bytes accessed | tf_op | source)
XLA Modules:
  0.0 13.6 jit_solution(18137979063455534450)
XLA Ops:
  0.0 0.0 copy-start
  0.0 0.0 copy-start.1
  0.0 0.0 copy-start.2
  0.0 0.0 copy-start.3
  0.0 0.0 copy-start.4
  0.0 0.0 copy-start.5
  0.0 0.0 copy-start.6
  0.0 0.0 copy-start.7
  0.0 0.9 %copy.10.mol_ref = f32[112,8]{1,0:T(8,128)S(1)} copy(f32[112,8]{0,1:T(8,128)} %param.13) | data formatting | bytes 7168 | tf_op args[4]
  0.9 0.0 copy-done
  0.9 0.0 copy-done.1
  0.9 0.0 copy-done.2
  0.9 0.0 copy-done.3
  0.9 0.0 copy-done.4
  1.0 0.0 copy-done.5
  1.0 0.0 copy-done.6
  1.0 0.0 copy-done.7
  1.0 12.0 %shard_map.91 = f32[2,16,512]{2,1,0:T(8,128)S(1)} custom-call(f32[2,1,256]{2,1,0:T(1,128)S(1)} %copy-done.2, f32[2,1,256]{2,1,0:T(1,128)S(1)} %copy-done.3, f32[2,1,256]{2,1,0:T(1,128)S(1)} %copy-done.4, s32[2,256]{1,0:T(2,128)S(1)} %copy-done.5, f32[112,8]{1,0:T(8,128)S(1)} %copy.10.mol_ref, f32[1,112]{1,0:T(1,128)S(1)} %bitcast.2, f32[1,112]{1,0:T(1,128)S(1)} %bitcast.3, ...), custom_call_target="tpu_custom_call" | custom-call | tf_op jit(solution)/shard_map/pallas_call | solution.py:235
  12.9 0.6 %copy.12 = f32[2,16,512]{2,1,0:T(8,128)} copy(f32[2,16,512]{2,1,0:T(8,128)S(1)} %shard_map.91) | data formatting | bytes 131072
Async XLA Ops:
  0.0 0.9 %copy-start = (s32[4,512]{1,0:T(4,128)S(1)}, s32[4,512]{1,0:T(4,128)}, u32[]{:S(2)}) copy-start(s32[4,512]{1,0:T(4,128)} %src_ref.1) | copy-start | bytes 24580
  0.0 0.9 %copy-start.1 = (f32[4,512]{1,0:T(4,128)S(1)}, f32[4,512]{1,0:T(4,128)}, u32[]{:S(2)}) copy-start(f32[4,512]{1,0:T(4,128)} %w_ref.1) | copy-start | bytes 24580
  0.0 0.9 %copy-start.2 = (f32[2,1,256]{2,1,0:T(1,128)S(1)}, f32[2,1,256]{2,1,0:T(1,128)}, u32[]{:S(2)}) copy-start(f32[2,1,256]{2,1,0:T(1,128)} %t_ref.1) | copy-start | bytes 6148
  0.0 0.9 %copy-start.3 = (f32[2,1,256]{2,1,0:T(1,128)S(1)}, f32[2,1,256]{2,1,0:T(1,128)}, u32[]{:S(2)}) copy-start(f32[2,1,256]{2,1,0:T(1,128)} %q_ref.1) | copy-start | bytes 6148
  0.0 0.9 %copy-start.4 = (f32[2,1,256]{2,1,0:T(1,128)S(1)}, f32[2,1,256]{2,1,0:T(1,128)}, u32[]{:S(2)}) copy-start(f32[2,1,256]{2,1,0:T(1,128)} %c_ref.1) | copy-start | bytes 6148
  0.0 0.9 %copy-start.5 = (s32[2,256]{1,0:T(2,128)S(1)}, s32[2,256]{1,0:T(2,128)}, u32[]{:S(2)}) copy-start(s32[2,256]{1,0:T(2,128)} %o_ref.1) | copy-start | bytes 6148
  0.0 0.9 %copy-start.6 = (f32[112]{0:T(128)S(1)}, f32[112]{0:T(128)}, u32[]{:S(2)}) copy-start(f32[112]{0:T(128)} %param.14) | copy-start | bytes 1348
  0.0 0.9 %copy-start.7 = (f32[112]{0:T(128)S(1)}, f32[112]{0:T(128)}, u32[]{:S(2)}) copy-start(f32[112]{0:T(128)} %param.15) | copy-start | bytes 1348
